TPU v7x, 1024 devices: a whole 8x8x8 slice. The times are simulated.
1024 devices in a mesh: comp: 16 (over z, core), lat: 64 (over y, x).
Axes of the slice: x: 8, y: 8, z: 8, core: 2. Of those that a mesh axis runs over, the one named last changes fastest.
Arguments:
- spectrum: float32 [1152, 128, 2048], P('comp', 'lat'), may hold values from 0.1 to 2
- courant_lat: float32 [1152], P('comp'), may hold values from -0.45 to 0.45
- courant_lon: float32 [1152], P('comp'), may hold values from -0.45 to 0.45
- sea_mask: int32 [128, 2048], P('lat'), may hold values from 0 to 1, as said below
- strength: float32 [1152], replicated, may hold values from 0.02 to 0.2
- quad_shift: int32 [4, 2], replicated, may hold values from -4 to 4
Outputs:
- spectrum_next: float32 [1152, 128, 2048], P('comp', 'lat')
Inputs may be any that keep to these rules, and one draw needn't show every extreme that they name: `quad_shift`: column 0 offsets frequency, column 1 offsets direction. `sea_mask`: each aligned block of 2 rows holds at most 3072 sea points, and some block holds exactly 3072.
All inputs are finite; a program needn't handle non-finite values.
Results may differ from a plain program's by a relative error of at most 0.00002.
Values sent between devices are 32-bit elements; how exact they have to be, the bound alone decides.
A program may use at most 32 MiB of HBM per device.

v0:
```python
import jax
import jax.numpy as jnp
from jax import lax
from jax.sharding import PartitionSpec as P

NF = 36
ND = 32
NQ = 4


reach = 4


def extended(cells, sides, width):
    for axis, dim in sides:
        count = lax.axis_size(axis)
        ends = count - 1
        head = lax.slice_in_dim(cells, 0, width, axis=dim)
        tail = lax.slice_in_dim(cells, cells.shape[dim] - width, cells.shape[dim], axis=dim)
        cells = jnp.concatenate(
            [
                lax.ppermute(tail, axis, [(i, (i + 1) % count) for i in range(ends)]),
                cells,
                lax.ppermute(head, axis, [((i + 1) % count, i) for i in range(ends)]),
            ],
            axis=dim,
        )
    return cells


def upwind(field, along_lat, along_lon, maskf):
    padded = extended(field, (("lat", 1),), 1)
    south = padded[:, :-2, :]
    north = padded[:, 2:, :]
    west = jnp.roll(field, 1, axis=2)
    east = jnp.roll(field, -1, axis=2)
    plus_a = jnp.maximum(along_lat, 0.0)
    minus_a = jnp.minimum(along_lat, 0.0)
    plus_b = jnp.maximum(along_lon, 0.0)
    minus_b = jnp.minimum(along_lon, 0.0)
    moved = field - plus_a * (field - south) - minus_a * (north - field)
    moved = moved - plus_b * (field - west) - minus_b * (east - field)
    return moved * maskf


def interact(energy, strength, quad_shift):
    rest = energy.shape[1:]
    grid = energy.reshape((NF, ND) + rest)
    widths = ((reach, reach),) + ((0, 0),) * (grid.ndim - 1)
    padded = jnp.pad(grid, widths)
    total = jnp.zeros(grid.shape, jnp.float32)
    for index in range(NQ):
        offset_f = quad_shift[index, 0]
        offset_d = quad_shift[index, 1]
        partner = lax.dynamic_slice_in_dim(padded, reach + offset_f, NF, 0)
        partner = jnp.roll(partner, -offset_d, axis=1)
        total = total + partner * (partner - grid)
    coeff = strength.reshape((NF, ND) + (1,) * len(rest))
    return (coeff * grid * total).reshape(energy.shape)


def per_device(spectrum, courant_lat, courant_lon, sea_mask, strength, quad_shift):
    maskf = sea_mask.astype(jnp.float32)[None]
    along_lat = courant_lat[:, None, None]
    along_lon = courant_lon[:, None, None]
    field = upwind(spectrum, along_lat, along_lon, maskf)
    field = upwind(field, along_lat, along_lon, maskf)
    comp_dev, lat_dev, lon_count = field.shape
    point_count = lat_dev * lon_count
    flat = field.reshape(comp_dev, point_count)
    spectra = lax.all_to_all(flat, "comp", split_axis=1, concat_axis=0, tiled=True)
    updated = spectra + interact(spectra, strength, quad_shift)
    result = lax.all_to_all(updated, "comp", split_axis=0, concat_axis=1, tiled=True)
    return result.reshape(comp_dev, lat_dev, lon_count)


def solution(mesh):
    return jax.shard_map(
        per_device,
        mesh=mesh,
        in_specs=(P("comp", "lat", None), P("comp"), P("comp"), P("lat", None), P(), P()),
        out_specs=P("comp", "lat", None),
        check_vma=False,
    )
```

profile of v0, /device:TPU:63, one launch (start us, length us, event | category | flops | bytes accessed | tf_op | source)
XLA Modules:
  0.0 141.0 jit_solution(8003853797038221788)
XLA Ops:
  0.0 2.0 %copy.12 = f32[72,2,2048]{2,0,1:T(8,128)S(1)} copy(f32[72,2,2048]{2,1,0:T(2,128)} %param.8) | data formatting | bytes 2359296 | tf_op args[0]
  2.0 0.0 copy-start.3
  2.0 0.0 copy-start.4
  2.0 0.1 fusion.35
  2.1 4.3 %collective-permute-start = (f32[72,1,2048]{2,0,1:T(8,128)S(1)}, f32[72,1,2048]{2,0,1:T(8,128)S(1)}, u32[]{:S(2)}, u32[]{:S(2)}) collective-permute-start(f32[72,1,2048]{2,0,1:T(8,128)S(1)} %get-tuple-element.20), channel_id=1, source_target_pairs={{0,1},{1,2},{2,3},{3,4},{4,5},{5,6},{6,7},{7,8},{8,9},{9,10},{10,1... | collective-permute-start | bytes 1769480 | tf_op jit(solution)/shard_map/ppermute | solution.py:22
  6.4 1.9 %collective-permute-start.1 = (f32[72,1,2048]{2,0,1:T(8,128)S(1)}, f32[72,1,2048]{2,0,1:T(8,128)S(1)}, u32[]{:S(2)}, u32[]{:S(2)}) collective-permute-start(f32[72,1,2048]{2,0,1:T(8,128)S(1)} %get-tuple-element.21), channel_id=1, source_target_pairs={{1,0},{2,1},{3,2},{4,3},{5,4},{6,5},{7,6},{8,7},{9,8},{10,9},{11,1... | collective-permute-start | bytes 1769480 | tf_op jit(solution)/shard_map/ppermute | solution.py:24
  8.4 0.1 fusion.34
  8.5 0.4 fusion.33
  8.9 9.5 %collective-permute-done = f32[72,1,2048]{2,0,1:T(8,128)S(1)} collective-permute-done((f32[72,1,2048]{2,0,1:T(8,128)S(1)}, f32[72,1,2048]{2,0,1:T(8,128)S(1)}, u32[]{:S(2)}, u32[]{:S(2)}) %collective-permute-start) | collective-permute-done | bytes 589856 | tf_op jit(solution)/shard_map/ppermute | solution.py:22
  18.4 7.1 %collective-permute-done.1 = f32[72,1,2048]{2,0,1:T(8,128)S(1)} collective-permute-done((f32[72,1,2048]{2,0,1:T(8,128)S(1)}, f32[72,1,2048]{2,0,1:T(8,128)S(1)}, u32[]{:S(2)}, u32[]{:S(2)}) %collective-permute-start.1) | collective-permute-done | bytes 589856 | tf_op jit(solution)/shard_map/ppermute | solution.py:24
  25.5 0.7 fusion.22
  26.3 0.1 fusion.32
  26.4 1.9 %collective-permute-start.2 = (f32[72,1,2048]{2,0,1:T(8,128)S(1)}, f32[72,1,2048]{2,0,1:T(8,128)S(1)}, u32[]{:S(2)}, u32[]{:S(2)}) collective-permute-start(f32[72,1,2048]{2,0,1:T(8,128)S(1)} %get-tuple-element.14), channel_id=1, source_target_pairs={{0,1},{1,2},{2,3},{3,4},{4,5},{5,6},{6,7},{7,8},{8,9},{9,10},{10,1... | collective-permute-start | bytes 1769480 | tf_op jit(solution)/shard_map/ppermute | solution.py:22
  28.3 3.4 %collective-permute-start.3 = (f32[72,1,2048]{2,0,1:T(8,128)S(1)}, f32[72,1,2048]{2,0,1:T(8,128)S(1)}, u32[]{:S(2)}, u32[]{:S(2)}) collective-permute-start(f32[72,1,2048]{2,0,1:T(8,128)S(1)} %get-tuple-element.15), channel_id=1, source_target_pairs={{1,0},{2,1},{3,2},{4,3},{5,4},{6,5},{7,6},{8,7},{9,8},{10,9},{11,1... | collective-permute-start | bytes 1769480 | tf_op jit(solution)/shard_map/ppermute | solution.py:24
  31.7 0.1 fusion.31
  31.7 0.4 fusion.30
  32.2 9.1 %collective-permute-done.2 = f32[72,1,2048]{2,0,1:T(8,128)S(1)} collective-permute-done((f32[72,1,2048]{2,0,1:T(8,128)S(1)}, f32[72,1,2048]{2,0,1:T(8,128)S(1)}, u32[]{:S(2)}, u32[]{:S(2)}) %collective-permute-start.2) | collective-permute-done | bytes 589856 | tf_op jit(solution)/shard_map/ppermute | solution.py:22
  41.2 5.2 %collective-permute-done.3 = f32[72,1,2048]{2,0,1:T(8,128)S(1)} collective-permute-done((f32[72,1,2048]{2,0,1:T(8,128)S(1)}, f32[72,1,2048]{2,0,1:T(8,128)S(1)}, u32[]{:S(2)}, u32[]{:S(2)}) %collective-permute-start.3) | collective-permute-done | bytes 589856 | tf_op jit(solution)/shard_map/ppermute | solution.py:24
  46.5 0.7 fusion.13
  47.2 0.9 copy.22
  48.1 0.9 all_to_all.22
  49.1 1.7 %copy.23 = f32[72,16,256]{2,0,1:T(8,128)} copy(f32[72,16,256]{2,1,0:T(8,128)S(1)} %all_to_all.22) | data formatting | bytes 2359296 | tf_op jit(solution)/shard_map/all_to_all | solution.py:71
  50.8 19.8 %all-to-all-start = ((f32[72,16,256]{2,0,1:T(8,128)}), f32[72,16,256]{2,0,1:T(8,128)S(1)}, u32[]{:S(2)}, u32[]{:S(2)}) async-start(f32[72,16,256]{2,0,1:T(8,128)} %copy.23), calls=%async_computation | async-start | bytes 2359296 | tf_op jit(solution)/shard_map/all_to_all | solution.py:71
  70.5 0.7 fusion.36
  79.1 0.1 mul.110
  79.2 21.9 %all-to-all-done = f32[72,16,256]{2,0,1:T(8,128)S(1)} async-done(((f32[72,16,256]{2,0,1:T(8,128)}), f32[72,16,256]{2,0,1:T(8,128)S(1)}, u32[]{:S(2)}, u32[]{:S(2)}) %all-to-all-start) | async-done | bytes 1179680 | tf_op jit(solution)/shard_map/all_to_all | solution.py:71
  101.1 0.6 pad_dynamic-slice_fusion.11
  101.7 2.1 %fusion.3 = f32[36,32,256]{2,1,0:T(8,128)S(1)} fusion(f32[36,32,256]{2,1,0:T(8,128)S(1)} %bitcast.19, s32[]{:T(128)S(6)} %select_n.39, f32[36,32,256]{2,1,0:T(8,128)S(1)} %get-tuple-element.9, s32[]{:T(128)S(6)} %select_n.37, f32[36,32,256]{2,1,0:T(8,128)S(1)} %get-tuple-element.7, s32[]{:T(128)S(6)} %select_n.35, f32[36,32,256]{2,1,0:T(8,128)S(1)} %get-tuple-element.8, ...), kind=kLoop, calls=%fused_computation.19 | loop fusion | flops 5013504 | bytes 7082512 | tf_op jit(solution)/shard_map/mul | solution.py:59
  103.8 0.2 bitcast_add_fusion
  103.9 35.0 %all_to_all.29 = f32[16,72,256]{2,1,0:T(8,128)S(1)} all-to-all(f32[16,72,256]{2,1,0:T(8,128)S(1)} %bitcast_add_fusion), channel_id=1, replica_groups=mesh['comp'=16,'lat'=64] {'comp'}, dimensions={0} | all-to-all | bytes 2359296 | tf_op jit(solution)/shard_map/all_to_all | solution.py:73
  138.9 0.4 copy.24
  139.3 1.7 %reshape.53 = f32[72,2,2048]{2,1,0:T(2,128)} reshape(f32[72,16,256]{2,1,0:T(8,128)S(1)} %copy.24) | data formatting | bytes 2359296 | tf_op jit(solution)/shard_map/reshape | solution.py:74
  (10 shorter events, 0.0 us)
Async XLA Ops:
  2.0 6.5 %copy-start.3 = (f32[72]{0:T(128)S(1)}, f32[72]{0:T(128)}, u32[]{:S(2)}) copy-start(f32[72]{0:T(128)} %param.10) | copy-start | bytes 868
  2.0 6.5 %copy-start.4 = (f32[72]{0:T(128)S(1)}, f32[72]{0:T(128)}, u32[]{:S(2)}) copy-start(f32[72]{0:T(128)} %param.9) | copy-start | bytes 868
  2.0 6.5 %copy-start = (s32[2,2048]{1,0:T(2,128)S(1)}, s32[2,2048]{1,0:T(2,128)}, u32[]{:S(2)}) copy-start(s32[2,2048]{1,0:T(2,128)} %param.11) | copy-start | bytes 49156
  2.1 16.3 %collective-permute-start = (f32[72,1,2048]{2,0,1:T(8,128)S(1)}, f32[72,1,2048]{2,0,1:T(8,128)S(1)}, u32[]{:S(2)}, u32[]{:S(2)}) collective-permute-start(f32[72,1,2048]{2,0,1:T(8,128)S(1)} %get-tuple-element.20), channel_id=1, source_target_pairs={{0,1},{1,2},{2,3},{3,4},{4,5},{5,6},{6,7},{7,8},{8,9},{9,10},{10,1... | collective-permute-start | bytes 1769480 | tf_op jit(solution)/shard_map/ppermute | solution.py:22
  6.4 19.1 %collective-permute-start.1 = (f32[72,1,2048]{2,0,1:T(8,128)S(1)}, f32[72,1,2048]{2,0,1:T(8,128)S(1)}, u32[]{:S(2)}, u32[]{:S(2)}) collective-permute-start(f32[72,1,2048]{2,0,1:T(8,128)S(1)} %get-tuple-element.21), channel_id=1, source_target_pairs={{1,0},{2,1},{3,2},{4,3},{5,4},{6,5},{7,6},{8,7},{9,8},{10,9},{11,1... | collective-permute-start | bytes 1769480 | tf_op jit(solution)/shard_map/ppermute | solution.py:24
  26.4 14.9 %collective-permute-start.2 = (f32[72,1,2048]{2,0,1:T(8,128)S(1)}, f32[72,1,2048]{2,0,1:T(8,128)S(1)}, u32[]{:S(2)}, u32[]{:S(2)}) collective-permute-start(f32[72,1,2048]{2,0,1:T(8,128)S(1)} %get-tuple-element.14), channel_id=1, source_target_pairs={{0,1},{1,2},{2,3},{3,4},{4,5},{5,6},{6,7},{7,8},{8,9},{9,10},{10,1... | collective-permute-start | bytes 1769480 | tf_op jit(solution)/shard_map/ppermute | solution.py:22
  28.3 18.2 %collective-permute-start.3 = (f32[72,1,2048]{2,0,1:T(8,128)S(1)}, f32[72,1,2048]{2,0,1:T(8,128)S(1)}, u32[]{:S(2)}, u32[]{:S(2)}) collective-permute-start(f32[72,1,2048]{2,0,1:T(8,128)S(1)} %get-tuple-element.15), channel_id=1, source_target_pairs={{1,0},{2,1},{3,2},{4,3},{5,4},{6,5},{7,6},{8,7},{9,8},{10,9},{11,1... | collective-permute-start | bytes 1769480 | tf_op jit(solution)/shard_map/ppermute | solution.py:24
  50.8 19.8 %copy-start.1 = (s32[4,2]{0,1:T(2,128)S(1)}, s32[4,2]{0,1:T(2,128)}, u32[]{:S(2)}) copy-start(s32[4,2]{0,1:T(2,128)} %param.13) | copy-start | bytes 100
  50.8 28.3 %copy-start.2 = (f32[1152]{0:T(1024)S(1)}, f32[1152]{0:T(1024)}, u32[]{:S(2)}) copy-start(f32[1152]{0:T(1024)} %param.12) | copy-start | bytes 13828
  50.8 50.3 %all-to-all-start = ((f32[72,16,256]{2,0,1:T(8,128)}), f32[72,16,256]{2,0,1:T(8,128)S(1)}, u32[]{:S(2)}, u32[]{:S(2)}) async-start(f32[72,16,256]{2,0,1:T(8,128)} %copy.23), calls=%async_computation | async-start | bytes 2359296 | tf_op jit(solution)/shard_map/all_to_all | solution.py:71
where the time goes:
time: 142 us; the launch traced here: 141 us
  waiting for transfers between devices  52.9 us (37%)
  blocking collectives  35 us (25%)
  starting transfers between devices  31.3 us (22%)
  local copies, waits for them, and re-layouts  10.2 us (7%)
  between operations  8.04 us (6%)
  other arithmetic  3.68 us (3%)
    all_to_all x1, blocking collectives, per_device(): lax.all_to_all(updated, 'comp', split_axis=0, concat_axis=1, tiled=True)  35 us
    all_to_all x1, waiting for transfers between devices, per_device(): lax.all_to_all(flat, 'comp', split_axis=1, concat_axis=0, tiled=True)  21.9 us
    all_to_all x1, starting transfers between devices, per_device(): lax.all_to_all(flat, 'comp', split_axis=1, concat_axis=0, tiled=True)  19.8 us
    ppermute x2, waiting for transfers between devices, extended(): lax.ppermute(tail, axis, [(i, (i + 1) % count) for i in range(ends)])  18.6 us
    ppermute x2, waiting for transfers between devices, extended(): lax.ppermute(head, axis, [((i + 1) % count, i) for i in range(ends)])  12.4 us
    ppermute x2, starting transfers between devices, extended(): lax.ppermute(tail, axis, [(i, (i + 1) % count) for i in range(ends)])  6.25 us
    ppermute x2, starting transfers between devices, extended(): lax.ppermute(head, axis, [((i + 1) % count, i) for i in range(ends)])  5.28 us
  transfers between devices with their start and end apart: 5, of which 5 were waited for; matrix products, arithmetic and copies ran while one was open for 1% of the time, Pallas kernels for 0%

commit v1 on v0

v1 whole, which is shorter than its diff:
```python
import functools

import jax
import jax.numpy as jnp
from jax import lax
from jax.experimental import pallas as pl
from jax.experimental.pallas import tpu as pltpu
from jax.sharding import PartitionSpec as P

NF = 36
ND = 32
NQ = 4
COMP = 72
CHIP = 2 * COMP
CHUNKS = 9
STEP = COMP // CHUNKS
PIECES = 3
PART = COMP // PIECES

MESH = pl.DeviceIdType.MESH


def roll_lon(e, edge_west, edge_east, low_sub, high_sub):
    down = pltpu.roll(e, 2, axis=1)
    down = jnp.where(low_sub, jnp.concatenate([down[3:], down[:3]], axis=0), down)
    west = pltpu.roll(jnp.where(edge_west, down, e), 1, axis=2)
    up = pltpu.roll(e, 6, axis=1)
    up = jnp.where(high_sub, jnp.concatenate([up[1:], up[:1]], axis=0), up)
    east = pltpu.roll(jnp.where(edge_east, up, e), 127, axis=2)
    return west, east


def kernel(
    n_comp,
    n_lat,
    x_ref,
    lat_ref,
    lon_ref,
    mask_ref,
    strength_ref,
    shift_ref,
    out_ref,
    xv,
    south,
    north,
    mask_south,
    mask_north,
    g,
    other,
    res_own,
    res_sib,
    load_sem,
    x_send,
    x_recv,
    m_send,
    m_recv,
    z_send,
    z_recv,
    swap_send,
    swap_recv,
    ret_send,
    ret_recv,
    out_sem,
):
    comp = lax.axis_index("comp")
    lat = lax.axis_index("lat")
    z = comp // 2
    core = comp % 2
    n_z = n_comp // 2
    has_south = lat > 0
    has_north = lat < n_lat - 1
    has_below = z > 0
    has_above = z < n_z - 1
    sib = z * 2 + 1 - core

    def rows(ch):
        return pl.ds(ch * STEP, STEP)

    def load(ch):
        return pltpu.make_async_copy(x_ref.at[rows(ch)], xv.at[rows(ch)], load_sem.at[ch])

    def to_north(ch):
        return pltpu.make_async_remote_copy(
            src_ref=x_ref.at[rows(ch)],
            dst_ref=south.at[rows(ch)],
            send_sem=x_send.at[0, ch],
            recv_sem=x_recv.at[0, ch],
            device_id={"lat": lat + 1},
            device_id_type=MESH,
        )

    def to_south(ch):
        return pltpu.make_async_remote_copy(
            src_ref=x_ref.at[rows(ch)],
            dst_ref=north.at[rows(ch)],
            send_sem=x_send.at[1, ch],
            recv_sem=x_recv.at[1, ch],
            device_id={"lat": lat - 1},
            device_id_type=MESH,
        )

    def mask_to_north():
        return pltpu.make_async_remote_copy(
            src_ref=mask_ref,
            dst_ref=mask_south,
            send_sem=m_send.at[0],
            recv_sem=m_recv.at[0],
            device_id={"lat": lat + 1},
            device_id_type=MESH,
        )

    def mask_to_south():
        return pltpu.make_async_remote_copy(
            src_ref=mask_ref,
            dst_ref=mask_north,
            send_sem=m_send.at[1],
            recv_sem=m_recv.at[1],
            device_id={"lat": lat - 1},
            device_id_type=MESH,
        )

    def half_src(h, ch):
        if h == 0:
            return g.at[pl.ds(CHIP + core * COMP + ch * STEP, STEP)]
        return other.at[rows(ch)]

    def to_z(direction, h, ch):
        third = 0 if direction == 0 else 2
        target = (z + 1 if direction == 0 else z - 1) * 2 + (core if h == 0 else 1 - core)
        return pltpu.make_async_remote_copy(
            src_ref=half_src(h, ch),
            dst_ref=g.at[pl.ds(third * CHIP + core * COMP + ch * STEP, STEP)],
            send_sem=z_send.at[direction, h, ch],
            recv_sem=z_recv.at[direction, core, ch],
            device_id={"comp": target},
            device_id_type=MESH,
        )

    def from_z(direction, source_core, ch):
        third = 0 if direction == 0 else 2
        here = g.at[pl.ds(third * CHIP + source_core * COMP + ch * STEP, STEP)]
        return pltpu.make_async_remote_copy(
            src_ref=here,
            dst_ref=here,
            send_sem=z_send.at[direction, 0, ch],
            recv_sem=z_recv.at[direction, source_core, ch],
            device_id={"comp": sib},
            device_id_type=MESH,
        )

    def swap(ch):
        return pltpu.make_async_remote_copy(
            src_ref=other.at[rows(ch)],
            dst_ref=g.at[pl.ds(CHIP + core * COMP + ch * STEP, STEP)],
            send_sem=swap_send.at[ch],
            recv_sem=swap_recv.at[ch],
            device_id={"comp": sib},
            device_id_type=MESH,
        )

    def swap_in(ch):
        here = g.at[pl.ds(CHIP + (1 - core) * COMP + ch * STEP, STEP)]
        return pltpu.make_async_remote_copy(
            src_ref=here,
            dst_ref=here,
            send_sem=swap_send.at[ch],
            recv_sem=swap_recv.at[ch],
            device_id={"comp": sib},
            device_id_type=MESH,
        )

    def give_back(piece):
        span = pl.ds(piece * PART, PART)
        return pltpu.make_async_remote_copy(
            src_ref=res_sib.at[span],
            dst_ref=out_ref.at[span, pl.ds(2 * core, 2)],
            send_sem=ret_send.at[piece],
            recv_sem=ret_recv.at[piece],
            device_id={"comp": sib},
            device_id_type=MESH,
        )

    def take_back(piece):
        span = pl.ds(piece * PART, PART)
        return pltpu.make_async_remote_copy(
            src_ref=res_sib.at[span],
            dst_ref=out_ref.at[span, pl.ds(2 * (1 - core), 2)],
            send_sem=ret_send.at[piece],
            recv_sem=ret_recv.at[piece],
            device_id={"comp": sib},
            device_id_type=MESH,
        )

    def write_own(piece):
        span = pl.ds(piece * PART, PART)
        return pltpu.make_async_copy(res_own.at[span], out_ref.at[span, pl.ds(2 * core, 2)], out_sem.at[piece])

    for ch in range(CHUNKS):
        load(ch).start()

    barrier = pltpu.get_barrier_semaphore()

    def greet(**where):
        pl.semaphore_signal(barrier, inc=1, device_id=where, device_id_type=MESH)

    greet(comp=sib)

    @pl.when(has_south)
    def _():
        greet(lat=lat - 1)

    @pl.when(has_north)
    def _():
        greet(lat=lat + 1)

    @pl.when(has_below)
    def _():
        greet(comp=2 * z - 2)
        greet(comp=2 * z - 1)

    @pl.when(has_above)
    def _():
        greet(comp=2 * z + 2)
        greet(comp=2 * z + 3)

    @pl.when(jnp.logical_not(has_south))
    def _():
        south[...] = jnp.zeros_like(south)
        mask_south[...] = jnp.zeros_like(mask_south)

    @pl.when(jnp.logical_not(has_north))
    def _():
        north[...] = jnp.zeros_like(north)
        mask_north[...] = jnp.zeros_like(mask_north)

    @pl.when(jnp.logical_not(has_below))
    def _():
        g[pl.ds(0, CHIP)] = jnp.zeros((CHIP, 2, 8, 128), jnp.float32)

    @pl.when(jnp.logical_not(has_above))
    def _():
        g[pl.ds(2 * CHIP, CHIP)] = jnp.zeros((CHIP, 2, 8, 128), jnp.float32)

    def one(flag):
        return flag.astype(jnp.int32)

    pl.semaphore_wait(barrier, 1 + one(has_south) + one(has_north) + 2 * (one(has_below) + one(has_above)))

    @pl.when(has_north)
    def _():
        mask_to_north().start()

    @pl.when(has_south)
    def _():
        mask_to_south().start()

    for ch in range(CHUNKS):

        @pl.when(has_north)
        def _():
            to_north(ch).start()

        @pl.when(has_south)
        def _():
            to_south(ch).start()

    @pl.when(has_south)
    def _():
        mask_to_north().wait_recv()

    @pl.when(has_north)
    def _():
        mask_to_south().wait_recv()

    shape = (4, 8, 128)
    lane = lax.broadcasted_iota(jnp.int32, shape, 2)
    sub = lax.broadcasted_iota(jnp.int32, shape, 1)
    edge_west = lane == 127
    edge_east = lane == 0
    low_sub = sub < 2
    high_sub = sub >= 6
    odd = (sub & 1) == 1

    def other_row(e):
        return jnp.where(odd, pltpu.roll(e, 1, axis=1), pltpu.roll(e, 7, axis=1))

    mask = mask_ref[...]
    for ch in range(CHUNKS):
        load(ch).wait()

        @pl.when(has_south)
        def _():
            to_north(ch).wait_recv()

        @pl.when(has_north)
        def _():
            to_south(ch).wait_recv()

        def propagate(i, carry):
            a = lat_ref[i]
            b = lon_ref[i]
            up = a > 0.0
            west_in = b > 0.0
            a = jnp.abs(a)
            b = jnp.abs(b)
            from_halo = odd == up

            def substep(e, upstream, m):
                west, east = roll_lon(e, edge_west, edge_east, low_sub, high_sub)
                side = jnp.where(west_in, west, east)
                moved = e - a * (e - upstream)
                moved = moved - b * (e - side)
                return moved * m

            e = xv[i]
            halo = jnp.where(up, south[i], north[i])
            halo_mask = jnp.where(up, mask_south[...], mask_north[...])
            first = substep(e, other_row(jnp.where(from_halo, halo, e)), mask)
            halo = substep(halo, other_row(halo), halo_mask)
            second = substep(first, other_row(jnp.where(from_halo, halo, first)), mask)
            mine = core == 0
            g[CHIP + core * COMP + i] = jnp.where(mine, second[:2], second[2:])
            other[i] = jnp.where(mine, second[2:], second[:2])
            return carry

        lax.fori_loop(ch * STEP, (ch + 1) * STEP, propagate, 0)

        for h in range(2):

            @pl.when(has_above)
            def _():
                to_z(0, h, ch).start()

            @pl.when(has_below)
            def _():
                to_z(1, h, ch).start()

        swap(ch).start()

    for ch in range(CHUNKS):
        swap_in(ch).wait_recv()
        for source_core in range(2):

            @pl.when(has_below)
            def _():
                from_z(0, source_core, ch).wait_recv()

            @pl.when(has_above)
            def _():
                from_z(1, source_core, ch).wait_recv()

    base = z * CHIP

    def source(i):
        k = base + i
        d = k & (ND - 1)
        e = g[CHIP + i]
        total = jnp.zeros_like(e)
        for q in range(NQ):
            place = CHIP + i - d + ND * shift_ref[q, 0] + ((d + shift_ref[q, 1]) & (ND - 1))
            partner = g[place]
            total = total + partner * (partner - e)
        return e + (strength_ref[k] * e) * total

    for piece in range(PIECES):

        def for_sibling(i, carry):
            res_sib[i] = source((1 - core) * COMP + i)
            return carry

        lax.fori_loop(piece * PART, (piece + 1) * PART, for_sibling, 0)
        give_back(piece).start()

    for piece in range(PIECES):

        def for_me(i, carry):
            res_own[i] = source(core * COMP + i)
            return carry

        lax.fori_loop(piece * PART, (piece + 1) * PART, for_me, 0)
        write_own(piece).start()

    for ch in range(CHUNKS):

        @pl.when(has_north)
        def _():
            to_north(ch).wait_send()

        @pl.when(has_south)
        def _():
            to_south(ch).wait_send()

        for h in range(2):

            @pl.when(has_above)
            def _():
                to_z(0, h, ch).wait_send()

            @pl.when(has_below)
            def _():
                to_z(1, h, ch).wait_send()

        swap(ch).wait_send()

    @pl.when(has_north)
    def _():
        mask_to_north().wait_send()

    @pl.when(has_south)
    def _():
        mask_to_south().wait_send()

    for piece in range(PIECES):
        give_back(piece).wait_send()
        take_back(piece).wait_recv()
        write_own(piece).wait()


def solution(mesh):
    n_comp, n_lat = mesh.shape["comp"], mesh.shape["lat"]
    block = pltpu.VMEM((COMP, 4, 8, 128), jnp.float32)
    half = pltpu.VMEM((COMP, 2, 8, 128), jnp.float32)
    small = pltpu.VMEM((4, 8, 128), jnp.float32)
    dma = pltpu.SemaphoreType.DMA

    def per_device(spectrum, courant_lat, courant_lon, sea_mask, strength, quad_shift):
        x = spectrum.reshape(COMP, 2, 16, 128).transpose(0, 2, 1, 3).reshape(COMP, 4, 8, 128)
        mask = sea_mask.astype(jnp.float32).reshape(2, 16, 128).transpose(1, 0, 2).reshape(4, 8, 128)
        smem = pl.BlockSpec(memory_space=pltpu.SMEM)
        out = pl.pallas_call(
            functools.partial(kernel, n_comp, n_lat),
            out_shape=jax.ShapeDtypeStruct((COMP, 4, 8, 128), jnp.float32),
            in_specs=[
                pl.BlockSpec(memory_space=pl.ANY),
                smem,
                smem,
                pl.BlockSpec(memory_space=pltpu.VMEM),
                smem,
                smem,
            ],
            out_specs=pl.BlockSpec(memory_space=pl.ANY),
            scratch_shapes=[
                block,
                block,
                block,
                small,
                small,
                pltpu.VMEM((3 * CHIP, 2, 8, 128), jnp.float32),
                half,
                half,
                half,
                dma((CHUNKS,)),
                dma((2, CHUNKS)),
                dma((2, CHUNKS)),
                dma((2,)),
                dma((2,)),
                dma((2, 2, CHUNKS)),
                dma((2, 2, CHUNKS)),
                dma((CHUNKS,)),
                dma((CHUNKS,)),
                dma((PIECES,)),
                dma((PIECES,)),
                dma((PIECES,)),
            ],
            compiler_params=pltpu.CompilerParams(
                collective_id=0, has_side_effects=True, vmem_limit_bytes=40 * 1024 * 1024
            ),
        )(x, courant_lat, courant_lon, mask, strength, quad_shift)
        return out.reshape(COMP, 16, 2, 128).transpose(0, 2, 1, 3).reshape(COMP, 2, 2048)

    return jax.shard_map(
        per_device,
        mesh=mesh,
        in_specs=(P("comp", "lat", None), P("comp"), P("comp"), P("lat", None), P(), P()),
        out_specs=P("comp", "lat", None),
        check_vma=False,
    )
```

time: 142 us -> 59.8 us (0.42)
  the two profiles are of different devices: /device:TPU:63 before, /device:TPU:3 now
where the time goes in v1:
time: 59.8 us; the launch traced here: 59.5 us
  Pallas kernels  53.7 us (90%)
  local copies, waits for them, and re-layouts  5.06 us (8%)
  other arithmetic  0.72 us (1%)
    pallas_call x1, Pallas kernels, per_device(): pl.pallas_call(functools.partial(kernel, n_comp, n_lat), out_shape=jax.Sh...  53.7 us
    unnamed x10, local copies, waits for them, and re-layouts  5.06 us

profile of v1, /device:TPU:3, one launch (start us, length us, event | category | flops | bytes accessed | tf_op | source)
XLA Modules:
  0.0 59.5 jit_solution(4274603049519816080)
XLA Ops:
  0.0 0.8 %copy.9.shift_ref = s32[4,2]{1,0:T(4,128)S(1)} copy(s32[4,2]{0,1:T(2,128)} %param.11) | data formatting | bytes 64 | tf_op args[5]
  0.8 0.7 %convert_element_type.3 = f32[2,2048]{1,0:T(2,128)S(1)} convert(s32[2,2048]{1,0:T(2,128)} %param.9) | non-fusion elementwise | flops 4096 | bytes 32768 | tf_op jit(solution)/shard_map/convert_element_type | solution.py:428
  1.5 0.0 copy-start
  1.5 1.3 %copy-done = f32[72,2,2048]{2,1,0:T(2,128)S(1)} copy-done((f32[72,2,2048]{2,1,0:T(2,128)S(1)}, f32[72,2,2048]{2,1,0:T(2,128)}, u32[]{:S(2)}) %copy-start) | copy-done | bytes 1179672
  2.8 0.0 copy-start.1
  2.8 0.7 %copy-done.1 = f32[1152]{0:T(1024)S(1)} copy-done((f32[1152]{0:T(1024)S(1)}, f32[1152]{0:T(1024)}, u32[]{:S(2)}) %copy-start.1) | copy-done | bytes 4632
  3.5 0.0 copy-start.2
  3.5 0.7 %copy-done.2 = f32[72]{0:T(128)S(1)} copy-done((f32[72]{0:T(128)S(1)}, f32[72]{0:T(128)}, u32[]{:S(2)}) %copy-start.2) | copy-done | bytes 312
  4.1 0.0 copy-start.3
  4.1 0.7 %copy-done.3 = f32[72]{0:T(128)S(1)} copy-done((f32[72]{0:T(128)S(1)}, f32[72]{0:T(128)}, u32[]{:S(2)}) %copy-start.3) | copy-done | bytes 312
  4.8 53.7 %shard_map.64 = f32[72,4,8,128]{3,2,1,0:T(8,128)S(1)} custom-call(f32[72,4,8,128]{3,2,1,0:T(8,128)S(1)} %bitcast.16, f32[72]{0:T(128)S(1)} %copy-done.2, f32[72]{0:T(128)S(1)} %copy-done.3, f32[4,8,128]{2,1,0:T(8,128)S(1)} %bitcast.17, f32[1152]{0:T(1024)S(1)} %copy-done.1, s32[4,2]{1,0:T(4,128)S(1)} %copy.9.shift_ref), custom_call_target="tpu_custom_call" | custom-call | tf_op jit(solution)/shard_map/pallas_call | solution.py:430
  58.5 1.0 %copy.12 = f32[72,2,2048]{2,1,0:T(2,128)} copy(f32[72,2,2048]{2,1,0:T(2,128)S(1)} %bitcast.15) | data formatting | bytes 2359296
Async XLA Ops:
  1.5 1.3 %copy-start = (f32[72,2,2048]{2,1,0:T(2,128)S(1)}, f32[72,2,2048]{2,1,0:T(2,128)}, u32[]{:S(2)}) copy-start(f32[72,2,2048]{2,1,0:T(2,128)} %param.6) | copy-start | bytes 3538948
  2.8 0.7 %copy-start.1 = (f32[1152]{0:T(1024)S(1)}, f32[1152]{0:T(1024)}, u32[]{:S(2)}) copy-start(f32[1152]{0:T(1024)} %strength_ref.1) | copy-start | bytes 13828
  3.5 0.7 %copy-start.2 = (f32[72]{0:T(128)S(1)}, f32[72]{0:T(128)}, u32[]{:S(2)}) copy-start(f32[72]{0:T(128)} %lat_ref.1) | copy-start | bytes 868
  4.1 0.7 %copy-start.3 = (f32[72]{0:T(128)S(1)}, f32[72]{0:T(128)}, u32[]{:S(2)}) copy-start(f32[72]{0:T(128)} %lon_ref.1) | copy-start | bytes 868

commit v2 on v1

--- a/solution.py
+++ b/solution.py
@@ -16,6 +16,9 @@
 STEP = COMP // CHUNKS
 PIECES = 3
 PART = COMP // PIECES
+VMEM_BYTES = 627 * 1024 * 1024 // 10
+ROW = 8
+FAR = (ROW + 1, 2 * ROW + 1, 3 * ROW + 1)
 
 MESH = pl.DeviceIdType.MESH
 
@@ -34,12 +37,18 @@
     n_comp,
     n_lat,
     x_ref,
+    lat_any,
+    lon_any,
+    mask_any,
+    strength_any,
+    shift_any,
+    out_ref,
     lat_ref,
     lon_ref,
-    mask_ref,
     strength_ref,
     shift_ref,
-    out_ref,
+    place_ref,
+    mask_ref,
     xv,
     south,
     north,
@@ -47,8 +56,8 @@
     mask_north,
     g,
     other,
-    res_own,
     res_sib,
+    arg_sem,
     load_sem,
     x_send,
     x_recv,
@@ -60,7 +69,6 @@
     swap_recv,
     ret_send,
     ret_recv,
-    out_sem,
 ):
     comp = lax.axis_index("comp")
     lat = lax.axis_index("lat")
@@ -101,7 +109,7 @@
 
     def mask_to_north():
         return pltpu.make_async_remote_copy(
-            src_ref=mask_ref,
+            src_ref=mask_any,
             dst_ref=mask_south,
             send_sem=m_send.at[0],
             recv_sem=m_recv.at[0],
@@ -111,7 +119,7 @@
 
     def mask_to_south():
         return pltpu.make_async_remote_copy(
-            src_ref=mask_ref,
+            src_ref=mask_any,
             dst_ref=mask_north,
             send_sem=m_send.at[1],
             recv_sem=m_recv.at[1],
@@ -191,38 +199,55 @@
             device_id_type=MESH,
         )
 
-    def write_own(piece):
-        span = pl.ds(piece * PART, PART)
-        return pltpu.make_async_copy(res_own.at[span], out_ref.at[span, pl.ds(2 * core, 2)], out_sem.at[piece])
-
+    fetches = [
+        pltpu.make_async_copy(source_ref, target_ref, arg_sem.at[place])
+        for place, (source_ref, target_ref) in enumerate(
+            (
+                (lat_any, lat_ref),
+                (lon_any, lon_ref),
+                (mask_any, mask_ref),
+                (strength_any, strength_ref),
+                (shift_any, shift_ref),
+            )
+        )
+    ]
+
+    barrier = pltpu.get_barrier_semaphore()
+
+    def greet(**where):
+        pl.semaphore_signal(barrier, inc=1, device_id=where, device_id_type=MESH)
+
+    greet(comp=sib)
+
+    @pl.when(has_south)
+    def _():
+        greet(lat=lat - 1)
+
+    @pl.when(has_north)
+    def _():
+        greet(lat=lat + 1)
+
+    for far in FAR:
+
+        @pl.when(jnp.logical_and(lat % ROW == 0, lat >= far))
+        def _():
+            greet(lat=lat - far)
+
+    @pl.when(has_below)
+    def _():
+        greet(comp=2 * z - 2)
+        greet(comp=2 * z - 1)
+
+    @pl.when(has_above)
+    def _():
+        greet(comp=2 * z + 2)
+        greet(comp=2 * z + 3)
+
+    for fetch in fetches:
+        fetch.start()
     for ch in range(CHUNKS):
         load(ch).start()
 
-    barrier = pltpu.get_barrier_semaphore()
-
-    def greet(**where):
-        pl.semaphore_signal(barrier, inc=1, device_id=where, device_id_type=MESH)
-
-    greet(comp=sib)
-
-    @pl.when(has_south)
-    def _():
-        greet(lat=lat - 1)
-
-    @pl.when(has_north)
-    def _():
-        greet(lat=lat + 1)
-
-    @pl.when(has_below)
-    def _():
-        greet(comp=2 * z - 2)
-        greet(comp=2 * z - 1)
-
-    @pl.when(has_above)
-    def _():
-        greet(comp=2 * z + 2)
-        greet(comp=2 * z + 3)
-
     @pl.when(jnp.logical_not(has_south))
     def _():
         south[...] = jnp.zeros_like(south)
@@ -244,7 +269,8 @@
     def one(flag):
         return flag.astype(jnp.int32)
 
-    pl.semaphore_wait(barrier, 1 + one(has_south) + one(has_north) + 2 * (one(has_below) + one(has_above)))
+    ahead = sum(one(lat + far < n_lat) for far in FAR) * one(lat % ROW == ROW - 1)
+    pl.semaphore_wait(barrier, ahead + 1 + one(has_south) + one(has_north) + 2 * (one(has_below) + one(has_above)))
 
     @pl.when(has_north)
     def _():
@@ -284,8 +310,20 @@
     def other_row(e):
         return jnp.where(odd, pltpu.roll(e, 1, axis=1), pltpu.roll(e, 7, axis=1))
 
-    mask = mask_ref[...]
-    for ch in range(CHUNKS):
+    for fetch in fetches:
+        fetch.wait()
+    mask = mask_ref[...].astype(jnp.float32)
+    base = z * CHIP
+
+    def places(i, carry):
+        d = (base + i) & (ND - 1)
+        for q in range(NQ):
+            place_ref[q, i] = CHIP + i - d + ND * shift_ref[0, q] + ((d + shift_ref[1, q]) & (ND - 1))
+        return carry
+
+    lax.fori_loop(0, CHIP, places, 0, unroll=2)
+
+    def advance(ch, carry):
         load(ch).wait()
 
         @pl.when(has_south)
@@ -296,7 +334,8 @@
         def _():
             to_south(ch).wait_recv()
 
-        def propagate(i, carry):
+        def propagate(j, carry):
+            i = ch * STEP + j
             a = lat_ref[i]
             b = lon_ref[i]
             up = a > 0.0
@@ -314,7 +353,7 @@
 
             e = xv[i]
             halo = jnp.where(up, south[i], north[i])
-            halo_mask = jnp.where(up, mask_south[...], mask_north[...])
+            halo_mask = jnp.where(up, mask_south[...], mask_north[...]).astype(jnp.float32)
             first = substep(e, other_row(jnp.where(from_halo, halo, e)), mask)
             halo = substep(halo, other_row(halo), halo_mask)
             second = substep(first, other_row(jnp.where(from_halo, halo, first)), mask)
@@ -323,7 +362,7 @@
             other[i] = jnp.where(mine, second[2:], second[:2])
             return carry
 
-        lax.fori_loop(ch * STEP, (ch + 1) * STEP, propagate, 0)
+        lax.fori_loop(0, STEP, propagate, 0, unroll=4)
 
         for h in range(2):
 
@@ -336,6 +375,9 @@
                 to_z(1, h, ch).start()
 
         swap(ch).start()
+        return carry
+
+    lax.fori_loop(0, CHUNKS, advance, 0)
 
     for ch in range(CHUNKS):
         swap_in(ch).wait_recv()
@@ -349,18 +391,13 @@
             def _():
                 from_z(1, source_core, ch).wait_recv()
 
-    base = z * CHIP
-
     def source(i):
-        k = base + i
-        d = k & (ND - 1)
         e = g[CHIP + i]
         total = jnp.zeros_like(e)
         for q in range(NQ):
-            place = CHIP + i - d + ND * shift_ref[q, 0] + ((d + shift_ref[q, 1]) & (ND - 1))
-            partner = g[place]
+            partner = g[place_ref[q, i]]
             total = total + partner * (partner - e)
-        return e + (strength_ref[k] * e) * total
+        return e + (strength_ref[base + i] * e) * total
 
     for piece in range(PIECES):
 
@@ -368,17 +405,14 @@
             res_sib[i] = source((1 - core) * COMP + i)
             return carry
 
-        lax.fori_loop(piece * PART, (piece + 1) * PART, for_sibling, 0)
+        lax.fori_loop(piece * PART, (piece + 1) * PART, for_sibling, 0, unroll=4)
         give_back(piece).start()
 
-    for piece in range(PIECES):
-
-        def for_me(i, carry):
-            res_own[i] = source(core * COMP + i)
-            return carry
-
-        lax.fori_loop(piece * PART, (piece + 1) * PART, for_me, 0)
-        write_own(piece).start()
+    def for_me(i, carry):
+        out_ref[i, pl.ds(2 * core, 2)] = source(core * COMP + i)
+        return carry
+
+    lax.fori_loop(0, COMP, for_me, 0, unroll=4)
 
     for ch in range(CHUNKS):
 
@@ -413,33 +447,30 @@
     for piece in range(PIECES):
         give_back(piece).wait_send()
         take_back(piece).wait_recv()
-        write_own(piece).wait()
 
 
 def solution(mesh):
     n_comp, n_lat = mesh.shape["comp"], mesh.shape["lat"]
     block = pltpu.VMEM((COMP, 4, 8, 128), jnp.float32)
     half = pltpu.VMEM((COMP, 2, 8, 128), jnp.float32)
-    small = pltpu.VMEM((4, 8, 128), jnp.float32)
+    small = pltpu.VMEM((4, 8, 128), jnp.int32)
     dma = pltpu.SemaphoreType.DMA
 
     def per_device(spectrum, courant_lat, courant_lon, sea_mask, strength, quad_shift):
         x = spectrum.reshape(COMP, 2, 16, 128).transpose(0, 2, 1, 3).reshape(COMP, 4, 8, 128)
-        mask = sea_mask.astype(jnp.float32).reshape(2, 16, 128).transpose(1, 0, 2).reshape(4, 8, 128)
-        smem = pl.BlockSpec(memory_space=pltpu.SMEM)
+        mask = sea_mask.reshape(2, 16, 128).transpose(1, 0, 2).reshape(4, 8, 128)
         out = pl.pallas_call(
             functools.partial(kernel, n_comp, n_lat),
-            out_shape=jax.ShapeDtypeStruct((COMP, 4, 8, 128), jnp.float32),
-            in_specs=[
-                pl.BlockSpec(memory_space=pl.ANY),
-                smem,
-                smem,
-                pl.BlockSpec(memory_space=pltpu.VMEM),
-                smem,
-                smem,
-            ],
-            out_specs=pl.BlockSpec(memory_space=pl.ANY),
+            out_shape=pltpu.VMEM((COMP, 4, 8, 128), jnp.float32),
+            in_specs=[pl.BlockSpec(memory_space=pltpu.HBM)] * 6,
+            out_specs=pl.BlockSpec(memory_space=pltpu.VMEM),
             scratch_shapes=[
+                pltpu.SMEM((COMP,), jnp.float32),
+                pltpu.SMEM((COMP,), jnp.float32),
+                pltpu.SMEM((NF * ND,), jnp.float32),
+                pltpu.SMEM((2, NQ), jnp.int32),
+                pltpu.SMEM((NQ, CHIP), jnp.int32),
+                small,
                 block,
                 block,
                 block,
@@ -448,7 +479,7 @@
                 pltpu.VMEM((3 * CHIP, 2, 8, 128), jnp.float32),
                 half,
                 half,
-                half,
+                dma((5,)),
                 dma((CHUNKS,)),
                 dma((2, CHUNKS)),
                 dma((2, CHUNKS)),
@@ -460,12 +491,11 @@
                 dma((CHUNKS,)),
                 dma((PIECES,)),
                 dma((PIECES,)),
-                dma((PIECES,)),
             ],
             compiler_params=pltpu.CompilerParams(
-                collective_id=0, has_side_effects=True, vmem_limit_bytes=40 * 1024 * 1024
+                collective_id=0, has_side_effects=True, vmem_limit_bytes=VMEM_BYTES
             ),
-        )(x, courant_lat, courant_lon, mask, strength, quad_shift)
+        )(x, courant_lat, courant_lon, mask, strength, quad_shift.T)
         return out.reshape(COMP, 16, 2, 128).transpose(0, 2, 1, 3).reshape(COMP, 2, 2048)
 
     return jax.shard_map(

time: 59.8 us -> 51 us (0.85)
  local copies, waits for them, and re-layouts: 5.06 us -> 1.02 us
  Pallas kernels: 53.7 us -> 49.8 us
  other arithmetic: 0.72 us -> 0 us
    unnamed x10 -> x1, local copies, waits for them, and re-layouts: 5.06 us -> 1.02 us
    pallas_call x1, Pallas kernels: 53.7 us -> 49.8 us  [per_device(): pl.pallas_call(functools.partial(kernel, n_comp, n_lat), out_shape=pltpu....]
    convert_element_type x1 -> x0, other arithmetic: 0.72 us -> none  [per_device(): sea_mask.astype(jnp.float32).reshape(2, 16, 128).transpose(1, 0, 2)]
where the time goes in v2:
time: 51 us; the launch traced here: 50.9 us
  Pallas kernels  49.8 us (98%)
  local copies, waits for them, and re-layouts  1.02 us (2%)
    pallas_call x1, Pallas kernels, per_device(): pl.pallas_call(functools.partial(kernel, n_comp, n_lat), out_shape=pltpu....  49.8 us

profile of v2, /device:TPU:3, one launch (start us, length us, event | category | flops | bytes accessed | tf_op | source)
XLA Modules:
  0.0 50.9 jit_solution(17742430152185288412)
XLA Ops:
  0.0 49.8 %shard_map.64 = f32[72,4,8,128]{3,2,1,0:T(8,128)S(1)} custom-call(f32[72,4,8,128]{3,2,1,0:T(8,128)} %bitcast.17, f32[72]{0:T(128)} %lat_any.1, f32[72]{0:T(128)} %lon_any.1, s32[4,8,128]{2,1,0:T(8,128)} %bitcast.18, f32[1152]{0:T(1024)} %strength_any.1, s32[2,4]{1,0:T(2,128)} %bitcast.19), custom_call_target="tpu_custom_call" | custom-call | tf_op jit(solution)/shard_map/pallas_call | solution.py:462
  49.8 1.0 %copy.11 = f32[72,2,2048]{2,1,0:T(2,128)} copy(f32[72,2,2048]{2,1,0:T(2,128)S(1)} %bitcast.16) | data formatting | bytes 2359296

commit v3 on v2

--- a/solution.py
+++ b/solution.py
@@ -18,6 +18,7 @@
 PART = COMP // PIECES
 VMEM_BYTES = 627 * 1024 * 1024 // 10
 ROW = 8
+HALF_WAY = 4 * ROW
 FAR = (ROW + 1, 2 * ROW + 1, 3 * ROW + 1)
 
 MESH = pl.DeviceIdType.MESH
@@ -69,6 +70,7 @@
     swap_recv,
     ret_send,
     ret_recv,
+    relay,
 ):
     comp = lax.axis_index("comp")
     lat = lax.axis_index("lat")
@@ -217,8 +219,6 @@
     def greet(**where):
         pl.semaphore_signal(barrier, inc=1, device_id=where, device_id_type=MESH)
 
-    greet(comp=sib)
-
     @pl.when(has_south)
     def _():
         greet(lat=lat - 1)
@@ -229,19 +229,9 @@
 
     for far in FAR:
 
-        @pl.when(jnp.logical_and(lat % ROW == 0, lat >= far))
+        @pl.when(jnp.logical_and(lat % ROW == 0, jnp.logical_and(lat >= far, lat <= HALF_WAY)))
         def _():
             greet(lat=lat - far)
-
-    @pl.when(has_below)
-    def _():
-        greet(comp=2 * z - 2)
-        greet(comp=2 * z - 1)
-
-    @pl.when(has_above)
-    def _():
-        greet(comp=2 * z + 2)
-        greet(comp=2 * z + 3)
 
     for fetch in fetches:
         fetch.start()
@@ -269,8 +259,22 @@
     def one(flag):
         return flag.astype(jnp.int32)
 
-    ahead = sum(one(lat + far < n_lat) for far in FAR) * one(lat % ROW == ROW - 1)
-    pl.semaphore_wait(barrier, ahead + 1 + one(has_south) + one(has_north) + 2 * (one(has_below) + one(has_above)))
+    near_z = 1 + one(has_below) + one(has_above)
+    ahead = sum(one(lat + far <= HALF_WAY) for far in FAR) * one(lat % ROW == ROW - 1)
+    odd_core = core == 1
+    pl.semaphore_wait(barrier, ahead + one(has_south) + one(has_north) + (1 - core) * near_z)
+
+    @pl.when(odd_core)
+    def _():
+        greet(comp=2 * z)
+
+        @pl.when(has_below)
+        def _():
+            greet(comp=2 * z - 2)
+
+        @pl.when(has_above)
+        def _():
+            greet(comp=2 * z + 2)
 
     @pl.when(has_north)
     def _():
@@ -289,6 +293,21 @@
         @pl.when(has_south)
         def _():
             to_south(ch).start()
+
+    def tell(target):
+        pl.semaphore_signal(relay, inc=1, device_id={"comp": target}, device_id_type=MESH)
+
+    @pl.when(core == 0)
+    def _():
+        tell(2 * z + 1)
+
+        @pl.when(has_below)
+        def _():
+            tell(2 * z - 1)
+
+        @pl.when(has_above)
+        def _():
+            tell(2 * z + 3)
 
     @pl.when(has_south)
     def _():
@@ -322,6 +341,12 @@
         return carry
 
     lax.fori_loop(0, CHIP, places, 0, unroll=2)
+
+    pl.semaphore_wait(relay, jnp.where(odd_core, near_z, 1))
+
+    @pl.when(odd_core)
+    def _():
+        tell(2 * z)
 
     def advance(ch, carry):
         load(ch).wait()
@@ -491,6 +516,7 @@
                 dma((CHUNKS,)),
                 dma((PIECES,)),
                 dma((PIECES,)),
+                pltpu.SemaphoreType.REGULAR,
             ],
             compiler_params=pltpu.CompilerParams(
                 collective_id=0, has_side_effects=True, vmem_limit_bytes=VMEM_BYTES

time: 51 us -> 48.8 us (0.957)
  the two profiles are of different devices: /device:TPU:3 before, /device:TPU:401 now
where the time goes in v3:
time: 48.8 us; the launch traced here: 48.7 us
  Pallas kernels  47.7 us (98%)
  local copies, waits for them, and re-layouts  1.02 us (2%)
    pallas_call x1, Pallas kernels, per_device(): pl.pallas_call(functools.partial(kernel, n_comp, n_lat), out_shape=pltpu....  47.7 us
    unnamed x1, local copies, waits for them, and re-layouts  1.02 us

profile of v3, /device:TPU:401, one launch (start us, length us, event | category | flops | bytes accessed | tf_op | source)
XLA Modules:
  0.0 48.7 jit_solution(18233014507749876241)
XLA Ops:
  0.0 47.7 %shard_map.64 = f32[72,4,8,128]{3,2,1,0:T(8,128)S(1)} custom-call(f32[72,4,8,128]{3,2,1,0:T(8,128)} %bitcast.17, f32[72]{0:T(128)} %lat_any.1, f32[72]{0:T(128)} %lon_any.1, s32[4,8,128]{2,1,0:T(8,128)} %bitcast.18, f32[1152]{0:T(1024)} %strength_any.1, s32[2,4]{1,0:T(2,128)} %bitcast.19), custom_call_target="tpu_custom_call" | custom-call | tf_op jit(solution)/shard_map/pallas_call | solution.py:487
  47.7 1.0 %copy.11 = f32[72,2,2048]{2,1,0:T(2,128)} copy(f32[72,2,2048]{2,1,0:T(2,128)S(1)} %bitcast.16) | data formatting | bytes 2359296

commit v4 on v2

--- a/solution.py
+++ b/solution.py
@@ -12,12 +12,16 @@
 NQ = 4
 COMP = 72
 CHIP = 2 * COMP
-CHUNKS = 9
-STEP = COMP // CHUNKS
+EDGE = 4
+STEP = 8
+MIDDLE = (COMP - 2 * EDGE) // STEP
+EARLY = 2
+CHUNKS = MIDDLE + 2
 PIECES = 3
 PART = COMP // PIECES
 VMEM_BYTES = 627 * 1024 * 1024 // 10
 ROW = 8
+HALF_WAY = 4 * ROW
 FAR = (ROW + 1, 2 * ROW + 1, 3 * ROW + 1)
 
 MESH = pl.DeviceIdType.MESH
@@ -69,6 +73,7 @@
     swap_recv,
     ret_send,
     ret_recv,
+    relay,
 ):
     comp = lax.axis_index("comp")
     lat = lax.axis_index("lat")
@@ -80,19 +85,38 @@
     has_below = z > 0
     has_above = z < n_z - 1
     sib = z * 2 + 1 - core
+    odd_core = core == 1
+
+    first_chunk = (0, 0, EDGE)
+    last_chunk = (CHUNKS - 1, COMP - EDGE, EDGE)
+
+    def middle_chunk(k):
+        return (k + 1, EDGE + STEP * k, STEP)
+
+    def each_chunk(act):
+        act(first_chunk)
+
+        def step(k, carry):
+            act(middle_chunk(k))
+            return carry
+
+        lax.fori_loop(0, MIDDLE, step, 0)
+        act(last_chunk)
+
+    def span_at(offset, ch):
+        return pl.ds(offset + ch[1], ch[2])
 
     def rows(ch):
-        return pl.ds(ch * STEP, STEP)
-
-    def load(ch):
-        return pltpu.make_async_copy(x_ref.at[rows(ch)], xv.at[rows(ch)], load_sem.at[ch])
+        return span_at(0, ch)
+
+    load = pltpu.make_async_copy(x_ref, xv, load_sem)
 
     def to_north(ch):
         return pltpu.make_async_remote_copy(
             src_ref=x_ref.at[rows(ch)],
             dst_ref=south.at[rows(ch)],
-            send_sem=x_send.at[0, ch],
-            recv_sem=x_recv.at[0, ch],
+            send_sem=x_send.at[0, ch[0]],
+            recv_sem=x_recv.at[0, ch[0]],
             device_id={"lat": lat + 1},
             device_id_type=MESH,
         )
@@ -101,8 +125,8 @@
         return pltpu.make_async_remote_copy(
             src_ref=x_ref.at[rows(ch)],
             dst_ref=north.at[rows(ch)],
-            send_sem=x_send.at[1, ch],
-            recv_sem=x_recv.at[1, ch],
+            send_sem=x_send.at[1, ch[0]],
+            recv_sem=x_recv.at[1, ch[0]],
             device_id={"lat": lat - 1},
             device_id_type=MESH,
         )
@@ -129,7 +153,7 @@
 
     def half_src(h, ch):
         if h == 0:
-            return g.at[pl.ds(CHIP + core * COMP + ch * STEP, STEP)]
+            return g.at[span_at(CHIP + core * COMP, ch)]
         return other.at[rows(ch)]
 
     def to_z(direction, h, ch):
@@ -137,21 +161,45 @@
         target = (z + 1 if direction == 0 else z - 1) * 2 + (core if h == 0 else 1 - core)
         return pltpu.make_async_remote_copy(
             src_ref=half_src(h, ch),
-            dst_ref=g.at[pl.ds(third * CHIP + core * COMP + ch * STEP, STEP)],
-            send_sem=z_send.at[direction, h, ch],
-            recv_sem=z_recv.at[direction, core, ch],
+            dst_ref=g.at[span_at(third * CHIP + core * COMP, ch)],
+            send_sem=z_send.at[direction, h, ch[0]],
+            recv_sem=z_recv.at[direction, core, ch[0]],
             device_id={"comp": target},
             device_id_type=MESH,
         )
+
+    def skipped(direction, parity, source_core, ch):
+        if direction == 0:
+            first = jnp.where(parity == 0, 4, 0)
+            last = 12
+            owner = 0
+        else:
+            first = 60
+            last = jnp.where(parity == 0, 72, 68)
+            owner = 1
+        start = ch[1]
+        return jnp.logical_and(source_core == owner, jnp.logical_and(start >= first, start < last))
+
+    def sends_up(ch):
+        return jnp.logical_and(has_above, jnp.logical_not(skipped(0, z % 2, core, ch)))
+
+    def sends_down(ch):
+        return jnp.logical_and(has_below, jnp.logical_not(skipped(1, z % 2, core, ch)))
+
+    def comes_up(source_core, ch):
+        return jnp.logical_and(has_below, jnp.logical_not(skipped(0, (z + 1) % 2, source_core, ch)))
+
+    def comes_down(source_core, ch):
+        return jnp.logical_and(has_above, jnp.logical_not(skipped(1, (z + 1) % 2, source_core, ch)))
 
     def from_z(direction, source_core, ch):
         third = 0 if direction == 0 else 2
-        here = g.at[pl.ds(third * CHIP + source_core * COMP + ch * STEP, STEP)]
+        here = g.at[span_at(third * CHIP + source_core * COMP, ch)]
         return pltpu.make_async_remote_copy(
             src_ref=here,
             dst_ref=here,
-            send_sem=z_send.at[direction, 0, ch],
-            recv_sem=z_recv.at[direction, source_core, ch],
+            send_sem=z_send.at[direction, 0, ch[0]],
+            recv_sem=z_recv.at[direction, source_core, ch[0]],
             device_id={"comp": sib},
             device_id_type=MESH,
         )
@@ -159,20 +207,20 @@
     def swap(ch):
         return pltpu.make_async_remote_copy(
             src_ref=other.at[rows(ch)],
-            dst_ref=g.at[pl.ds(CHIP + core * COMP + ch * STEP, STEP)],
-            send_sem=swap_send.at[ch],
-            recv_sem=swap_recv.at[ch],
+            dst_ref=g.at[span_at(CHIP + core * COMP, ch)],
+            send_sem=swap_send.at[ch[0]],
+            recv_sem=swap_recv.at[ch[0]],
             device_id={"comp": sib},
             device_id_type=MESH,
         )
 
     def swap_in(ch):
-        here = g.at[pl.ds(CHIP + (1 - core) * COMP + ch * STEP, STEP)]
+        here = g.at[span_at(CHIP + (1 - core) * COMP, ch)]
         return pltpu.make_async_remote_copy(
             src_ref=here,
             dst_ref=here,
-            send_sem=swap_send.at[ch],
-            recv_sem=swap_recv.at[ch],
+            send_sem=swap_send.at[ch[0]],
+            recv_sem=swap_recv.at[ch[0]],
             device_id={"comp": sib},
             device_id_type=MESH,
         )
@@ -217,7 +265,13 @@
     def greet(**where):
         pl.semaphore_signal(barrier, inc=1, device_id=where, device_id_type=MESH)
 
-    greet(comp=sib)
+    @pl.when(odd_core)
+    def _():
+        greet(comp=sib)
+
+    @pl.when(has_below)
+    def _():
+        greet(comp=2 * z - 2)
 
     @pl.when(has_south)
     def _():
@@ -229,24 +283,13 @@
 
     for far in FAR:
 
-        @pl.when(jnp.logical_and(lat % ROW == 0, lat >= far))
+        @pl.when(jnp.logical_and(jnp.logical_and(core == 0, lat % ROW == 0), jnp.logical_and(lat >= far, lat <= HALF_WAY)))
         def _():
             greet(lat=lat - far)
-
-    @pl.when(has_below)
-    def _():
-        greet(comp=2 * z - 2)
-        greet(comp=2 * z - 1)
-
-    @pl.when(has_above)
-    def _():
-        greet(comp=2 * z + 2)
-        greet(comp=2 * z + 3)
 
     for fetch in fetches:
         fetch.start()
-    for ch in range(CHUNKS):
-        load(ch).start()
+    load.start()
 
     @pl.when(jnp.logical_not(has_south))
     def _():
@@ -269,8 +312,22 @@
     def one(flag):
         return flag.astype(jnp.int32)
 
-    ahead = sum(one(lat + far < n_lat) for far in FAR) * one(lat % ROW == ROW - 1)
-    pl.semaphore_wait(barrier, ahead + 1 + one(has_south) + one(has_north) + 2 * (one(has_below) + one(has_above)))
+    ahead = sum(one(lat + far <= HALF_WAY) for far in FAR) * one(lat % ROW == ROW - 1)
+    held_back = jnp.logical_and(odd_core, ahead > 0)
+    line = one(has_south) + one(has_north)
+    pl.semaphore_wait(barrier, line + (1 - core) * (ahead + 1 + 2 * one(has_above)))
+
+    def tell(target):
+        pl.semaphore_signal(relay, inc=1, device_id={"comp": target}, device_id_type=MESH)
+
+    @pl.when(core == 0)
+    def _():
+        tell(2 * z + 1)
+
+        @pl.when(has_above)
+        def _():
+            tell(2 * z + 2)
+            tell(2 * z + 3)
 
     @pl.when(has_north)
     def _():
@@ -280,15 +337,21 @@
     def _():
         mask_to_south().start()
 
-    for ch in range(CHUNKS):
-
-        @pl.when(has_north)
+    def send_rows(ch):
+        @pl.when(jnp.logical_and(has_north, jnp.logical_or(jnp.logical_not(held_back), ch[0] <= EARLY)))
         def _():
             to_north(ch).start()
 
         @pl.when(has_south)
         def _():
             to_south(ch).start()
+
+    def send_rest(ch):
+        @pl.when(jnp.logical_and(held_back, ch[0] > EARLY))
+        def _():
+            to_north(ch).start()
+
+    each_chunk(send_rows)
 
     @pl.when(has_south)
     def _():
@@ -323,9 +386,15 @@
 
     lax.fori_loop(0, CHIP, places, 0, unroll=2)
 
-    def advance(ch, carry):
-        load(ch).wait()
-
+    @pl.when(jnp.logical_or(odd_core, has_below))
+    def _():
+        pl.semaphore_wait(relay, core + one(has_below))
+
+    each_chunk(send_rest)
+
+    load.wait()
+
+    def advance(ch):
         @pl.when(has_south)
         def _():
             to_north(ch).wait_recv()
@@ -335,7 +404,7 @@
             to_south(ch).wait_recv()
 
         def propagate(j, carry):
-            i = ch * STEP + j
+            i = ch[1] + j
             a = lat_ref[i]
             b = lon_ref[i]
             up = a > 0.0
@@ -362,34 +431,35 @@
             other[i] = jnp.where(mine, second[2:], second[:2])
             return carry
 
-        lax.fori_loop(0, STEP, propagate, 0, unroll=4)
+        lax.fori_loop(0, ch[2], propagate, 0, unroll=4)
 
         for h in range(2):
 
-            @pl.when(has_above)
+            @pl.when(sends_up(ch))
             def _():
                 to_z(0, h, ch).start()
 
-            @pl.when(has_below)
+            @pl.when(sends_down(ch))
             def _():
                 to_z(1, h, ch).start()
 
         swap(ch).start()
-        return carry
-
-    lax.fori_loop(0, CHUNKS, advance, 0)
-
-    for ch in range(CHUNKS):
+
+    each_chunk(advance)
+
+    def arrive(ch):
         swap_in(ch).wait_recv()
         for source_core in range(2):
 
-            @pl.when(has_below)
+            @pl.when(comes_up(source_core, ch))
             def _():
                 from_z(0, source_core, ch).wait_recv()
 
-            @pl.when(has_above)
+            @pl.when(comes_down(source_core, ch))
             def _():
                 from_z(1, source_core, ch).wait_recv()
+
+    each_chunk(arrive)
 
     def source(i):
         e = g[CHIP + i]
@@ -414,8 +484,7 @@
 
     lax.fori_loop(0, COMP, for_me, 0, unroll=4)
 
-    for ch in range(CHUNKS):
-
+    def left(ch):
         @pl.when(has_north)
         def _():
             to_north(ch).wait_send()
@@ -426,15 +495,17 @@
 
         for h in range(2):
 
-            @pl.when(has_above)
+            @pl.when(sends_up(ch))
             def _():
                 to_z(0, h, ch).wait_send()
 
-            @pl.when(has_below)
+            @pl.when(sends_down(ch))
             def _():
                 to_z(1, h, ch).wait_send()
 
         swap(ch).wait_send()
+
+    each_chunk(left)
 
     @pl.when(has_north)
     def _():
@@ -480,7 +551,7 @@
                 half,
                 half,
                 dma((5,)),
-                dma((CHUNKS,)),
+                dma,
                 dma((2, CHUNKS)),
                 dma((2, CHUNKS)),
                 dma((2,)),
@@ -491,6 +562,7 @@
                 dma((CHUNKS,)),
                 dma((PIECES,)),
                 dma((PIECES,)),
+                pltpu.SemaphoreType.REGULAR,
             ],
             compiler_params=pltpu.CompilerParams(
                 collective_id=0, has_side_effects=True, vmem_limit_bytes=VMEM_BYTES

time: 51 us -> 46.1 us (0.904)
  the two profiles are of different devices: /device:TPU:3 before, /device:TPU:1 now
where the time goes in v4:
time: 46.1 us; the launch traced here: 46 us
  Pallas kernels  45 us (98%)
  local copies, waits for them, and re-layouts  1.02 us (2%)
    pallas_call x1, Pallas kernels, per_device(): pl.pallas_call(functools.partial(kernel, n_comp, n_lat), out_shape=pltpu....  45 us
    unnamed x1, local copies, waits for them, and re-layouts  1.02 us

profile of v4, /device:TPU:1, one launch (start us, length us, event | category | flops | bytes accessed | tf_op | source)
XLA Modules:
  0.0 46.0 jit_solution(6552047679045392087)
XLA Ops:
  0.0 45.0 %shard_map.64 = f32[72,4,8,128]{3,2,1,0:T(8,128)S(1)} custom-call(f32[72,4,8,128]{3,2,1,0:T(8,128)} %bitcast.17, f32[72]{0:T(128)} %lat_any.1, f32[72]{0:T(128)} %lon_any.1, s32[4,8,128]{2,1,0:T(8,128)} %bitcast.18, f32[1152]{0:T(1024)} %strength_any.1, s32[2,4]{1,0:T(2,128)} %bitcast.19), custom_call_target="tpu_custom_call" | custom-call | tf_op jit(solution)/shard_map/pallas_call | solution.py:533
  45.0 1.0 %copy.11 = f32[72,2,2048]{2,1,0:T(2,128)} copy(f32[72,2,2048]{2,1,0:T(2,128)S(1)} %bitcast.16) | data formatting | bytes 2359296

commit v5 on v4

--- a/solution.py
+++ b/solution.py
@@ -269,9 +269,9 @@
     def _():
         greet(comp=sib)
 
-    @pl.when(has_below)
-    def _():
-        greet(comp=2 * z - 2)
+    @pl.when(has_above)
+    def _():
+        greet(comp=2 * z + 2)
 
     @pl.when(has_south)
     def _():
@@ -315,7 +315,7 @@
     ahead = sum(one(lat + far <= HALF_WAY) for far in FAR) * one(lat % ROW == ROW - 1)
     held_back = jnp.logical_and(odd_core, ahead > 0)
     line = one(has_south) + one(has_north)
-    pl.semaphore_wait(barrier, line + (1 - core) * (ahead + 1 + 2 * one(has_above)))
+    pl.semaphore_wait(barrier, line + (1 - core) * (ahead + 1 + 2 * one(has_below)))
 
     def tell(target):
         pl.semaphore_signal(relay, inc=1, device_id={"comp": target}, device_id_type=MESH)
@@ -324,10 +324,10 @@
     def _():
         tell(2 * z + 1)
 
-        @pl.when(has_above)
-        def _():
-            tell(2 * z + 2)
-            tell(2 * z + 3)
+        @pl.when(has_below)
+        def _():
+            tell(2 * z - 2)
+            tell(2 * z - 1)
 
     @pl.when(has_north)
     def _():
@@ -386,9 +386,9 @@
 
     lax.fori_loop(0, CHIP, places, 0, unroll=2)
 
-    @pl.when(jnp.logical_or(odd_core, has_below))
-    def _():
-        pl.semaphore_wait(relay, core + one(has_below))
+    @pl.when(jnp.logical_or(odd_core, has_above))
+    def _():
+        pl.semaphore_wait(relay, core + one(has_above))
 
     each_chunk(send_rest)
 

time: 46.1 us -> 46.3 us (level)
  no operation moved by 1% of the time
where the time goes in v5:
time: 46.3 us; the launch traced here: 46.1 us
  Pallas kernels  45.1 us (97%)
  local copies, waits for them, and re-layouts  1.02 us (2%)
    pallas_call x1, Pallas kernels, per_device(): pl.pallas_call(functools.partial(kernel, n_comp, n_lat), out_shape=pltpu....  45.1 us
    unnamed x1, local copies, waits for them, and re-layouts  1.02 us

profile of v5, /device:TPU:1, one launch (start us, length us, event | category | flops | bytes accessed | tf_op | source)
XLA Modules:
  0.0 46.1 jit_solution(10919659786494021326)
XLA Ops:
  0.0 45.1 %shard_map.64 = f32[72,4,8,128]{3,2,1,0:T(8,128)S(1)} custom-call(f32[72,4,8,128]{3,2,1,0:T(8,128)} %bitcast.17, f32[72]{0:T(128)} %lat_any.1, f32[72]{0:T(128)} %lon_any.1, s32[4,8,128]{2,1,0:T(8,128)} %bitcast.18, f32[1152]{0:T(1024)} %strength_any.1, s32[2,4]{1,0:T(2,128)} %bitcast.19), custom_call_target="tpu_custom_call" | custom-call | tf_op jit(solution)/shard_map/pallas_call | solution.py:533
  45.1 1.0 %copy.11 = f32[72,2,2048]{2,1,0:T(2,128)} copy(f32[72,2,2048]{2,1,0:T(2,128)S(1)} %bitcast.16) | data formatting | bytes 2359296

commit v6 on v4

--- a/solution.py
+++ b/solution.py
@@ -17,7 +17,7 @@
 MIDDLE = (COMP - 2 * EDGE) // STEP
 EARLY = 2
 CHUNKS = MIDDLE + 2
-PIECES = 3
+PIECES = 6
 PART = COMP // PIECES
 VMEM_BYTES = 627 * 1024 * 1024 // 10
 ROW = 8
@@ -433,6 +433,8 @@
 
         lax.fori_loop(0, ch[2], propagate, 0, unroll=4)
 
+        swap(ch).start()
+
         for h in range(2):
 
             @pl.when(sends_up(ch))
@@ -443,7 +445,6 @@
             def _():
                 to_z(1, h, ch).start()
 
-        swap(ch).start()
 
     each_chunk(advance)
 

time: 46.1 us -> 46.1 us (level)
  no operation moved by 1% of the time
where the time goes in v6:
time: 46.1 us; the launch traced here: 46 us
  Pallas kernels  44.9 us (97%)
  local copies, waits for them, and re-layouts  1.02 us (2%)
    pallas_call x1, Pallas kernels, per_device(): pl.pallas_call(functools.partial(kernel, n_comp, n_lat), out_shape=pltpu....  44.9 us
    unnamed x1, local copies, waits for them, and re-layouts  1.02 us

profile of v6, /device:TPU:1, one launch (start us, length us, event | category | flops | bytes accessed | tf_op | source)
XLA Modules:
  0.0 46.0 jit_solution(7794054103758101777)
XLA Ops:
  0.0 44.9 %shard_map.64 = f32[72,4,8,128]{3,2,1,0:T(8,128)S(1)} custom-call(f32[72,4,8,128]{3,2,1,0:T(8,128)} %bitcast.17, f32[72]{0:T(128)} %lat_any.1, f32[72]{0:T(128)} %lon_any.1, s32[4,8,128]{2,1,0:T(8,128)} %bitcast.18, f32[1152]{0:T(1024)} %strength_any.1, s32[2,4]{1,0:T(2,128)} %bitcast.19), custom_call_target="tpu_custom_call" | custom-call | tf_op jit(solution)/shard_map/pallas_call | solution.py:534
  44.9 1.0 %copy.11 = f32[72,2,2048]{2,1,0:T(2,128)} copy(f32[72,2,2048]{2,1,0:T(2,128)S(1)} %bitcast.16) | data formatting | bytes 2359296
